TPU v7x, 256 devices: a whole 4x4x8 slice. The times are simulated.
256 devices in a mesh: wide: 32 (over y_lo, z, core), narrow: 8 (over y_hi, x).
Axes of the slice: x: 4, y: 4 (y_hi: 2, y_lo: 2; y = y_hi * 2 + y_lo), z: 8, core: 2. Of those that a mesh axis runs over, the one named last changes fastest.
Arguments:
- tokens: bfloat16 [512, 16384], P('wide', 'narrow'), may hold values from -6 to 6
- gate_codes: bfloat16 [16384, 28672], P('narrow', 'wide'), may hold values from -6 to 6
- gate_scale: float32 [128, 224], P('narrow', 'wide'), may hold values from 0.00234375 to 0.0234375
- up_codes: bfloat16 [16384, 28672], P('narrow', 'wide'), may hold values from -6 to 6
- up_scale: float32 [128, 224], P('narrow', 'wide'), may hold values from 0.00234375 to 0.0234375
- down_codes: bfloat16 [28672, 16384], P('wide', 'narrow'), may hold values from -6 to 6
- down_scale: float32 [224, 128], P('wide', 'narrow'), may hold values from 0.0017717085 to 0.017717084
Outputs:
- mixed: bfloat16 [512, 16384], P('wide', 'narrow')
All inputs are finite; a program needn't handle non-finite values.
Results may differ from a plain program's by a relative error of at most 0.03.
Values may be sent and summed in bfloat16 or wider, within the bound.
A program may use at most 64 MiB of HBM per device.

v0:
```python
import jax
import jax.numpy as jnp
from jax import lax
from jax.sharding import PartitionSpec as P


def dequantize(codes, scale):
    height, breadth = codes.shape
    side = height // scale.shape[0]
    blocks = codes.astype(jnp.float32).reshape(scale.shape[0], side, scale.shape[1], side)
    return (blocks * scale[:, None, :, None]).reshape(height, breadth).astype(jnp.bfloat16)


def per_device(tokens, gate_codes, gate_scale, up_codes, up_scale, down_codes, down_scale):
    gate_weight = dequantize(gate_codes, gate_scale)
    up_weight = dequantize(up_codes, up_scale)
    down_weight = dequantize(down_codes, down_scale)
    joined = jnp.concatenate([gate_weight, up_weight], axis=1)
    units = gate_weight.shape[1]
    partial_sums = jnp.dot(
        lax.all_gather(tokens, "wide", axis=0, tiled=True),
        joined,
        preferred_element_type=jnp.float32,
    )
    summed = lax.psum(partial_sums, "narrow")
    hidden = (jax.nn.silu(summed[:, :units]) * summed[:, units:]).astype(jnp.bfloat16)
    return lax.psum_scatter(
        jnp.dot(hidden, down_weight, preferred_element_type=jnp.float32).astype(jnp.bfloat16),
        "wide",
        scatter_dimension=0,
        tiled=True,
    )


def solution(mesh):
    return jax.shard_map(
        per_device,
        mesh=mesh,
        in_specs=(
            P("wide", "narrow"),
            P("narrow", "wide"),
            P("narrow", "wide"),
            P("narrow", "wide"),
            P("narrow", "wide"),
            P("wide", "narrow"),
            P("wide", "narrow"),
        ),
        out_specs=P("wide", "narrow"),
        check_vma=False,
    )
```

profile of v0, /device:TPU:1, one launch (start us, length us, event | category | flops | bytes accessed | tf_op | source)
XLA Modules:
  0.0 324.9 jit_solution(9740533424817042235)
XLA Ops:
  6.5 0.0 all-gather.2.cloned.1.call-start
  6.5 0.7 all-gather.2.cloned.1.call-update
  7.3 0.0 all-reduce.2.cloned.1.call-start
  7.3 6.1 %copy.10 = bf16[2048,896]{0,1:T(8,128)(2,1)} copy(bf16[2048,896]{1,0:T(8,128)(2,1)} %param.8) | data formatting | bytes 7340032 | tf_op args[1]
  13.4 0.0 copy-start.2
  13.4 6.2 %copy.11 = bf16[2048,896]{0,1:T(8,128)(2,1)} copy(bf16[2048,896]{1,0:T(8,128)(2,1)} %param.10) | data formatting | bytes 7340032 | tf_op args[3]
  19.6 0.0 copy-done.2
  19.6 0.0 copy-start.3
  19.6 0.5 mul.40
  20.2 0.1 copy-done.3
  20.3 0.0 copy-start
  20.3 0.0 copy-start.1
  20.3 0.5 mul.43
  20.9 1.5 copy-done
  22.3 1.1 copy-done.1
  23.5 8.0 %fusion.1 = (bf16[2048,896]{0,1:T(8,128)(2,1)}, bf16[2048,896]{0,1:T(8,128)(2,1)}) fusion(f32[112,8,16,128]{3,2,1,0:T(8,128)S(1)} %bitcast.29, bf16[2048,896]{0,1:T(8,128)(2,1)S(1)} %copy-done.1, f32[112,8,16,128]{3,2,1,0:T(8,128)S(1)} %bitcast.28, bf16[2048,896]{0,1:T(8,128)(2,1)S(1)} %copy-done), kind=kLoop, calls=%fused_computation.3 | loop fusion | flops 11010048 | bytes 29360128 | tf_op jit(solution)/shard_map/convert_element_type | solution.py:11
  31.5 46.7 %all-gather.2.cloned.1.call-done = bf16[512,2048]{1,0:T(8,128)(2,1)} async-done(((bf16[16,2048]{1,0:T(8,128)(2,1)}), bf16[512,2048]{1,0:T(8,128)(2,1)}) %all-gather.2.cloned.1.call-update) | async-done | bytes 2097168 | tf_op jit(solution)/shard_map/all_gather | solution.py:21
  78.1 9.6 %fusion.9 = f32[512,1792]{0,1:T(8,128)} fusion(bf16[512,2048]{1,0:T(8,128)(2,1)} %all-gather.2.cloned.1.call-done, bf16[2048,896]{0,1:T(8,128)(2,1)} %get-tuple-element.5, bf16[2048,896]{0,1:T(8,128)(2,1)} %get-tuple-element.6), kind=kOutput, calls=%fused_computation.11 | convolution fusion | flops 3772776448 | bytes 13107200 | tf_op jit(solution)/shard_map/dot_general | solution.py:20
  87.7 0.0 copy-start.4
  87.7 0.0 all-reduce.2.cloned.1.call-update
  87.7 0.2 reduce-scatter.2.cloned.1.call-start
  88.0 105.4 %all-reduce.2.cloned.1.call-done = f32[512,1792]{0,1:T(8,128)} async-done(((f32[512,1792]{0,1:T(8,128)}), f32[512,1792]{0,1:T(8,128)}) %all-reduce.2.cloned.1.call-update) | async-done | bytes 3670032 | tf_op jit(solution)/shard_map/psum | solution.py:25
  193.3 0.0 copy-done.4
  193.3 0.0 copy-start.5
  193.3 0.0 copy-start.6
  193.3 0.5 mul.48
  193.9 1.5 copy-done.5
  195.4 1.1 copy-done.6
  196.5 5.5 %fusion.12 = bf16[512,2048]{1,0:T(8,128)(2,1)} fusion(f32[112,8,16,128]{3,2,1,0:T(8,128)S(1)} %bitcast.30, bf16[896,2048]{1,0:T(8,128)(2,1)S(1)} %copy-done.5, f32[512,1792]{0,1:T(8,128)S(1)} %copy-done.6), kind=kOutput, calls=%fused_computation.12 | convolution fusion | flops 1888354304 | bytes 16777216 | tf_op jit(solution)/shard_map/dot_general | solution.py:28
  202.0 0.0 reduce-scatter.2.cloned.1.call-update
  202.0 116.3 %reduce-scatter.2.cloned.1.call-done = bf16[16,2048]{1,0:T(8,128)(2,1)} async-done(((bf16[512,2048]{1,0:T(8,128)(2,1)}), bf16[16,2048]{1,0:T(8,128)(2,1)}) %reduce-scatter.2.cloned.1.call-update) | async-done | bytes 65552 | tf_op jit(solution)/shard_map/reduce_scatter | solution.py:27
Async XLA Ops:
  6.5 71.6 %all-gather.2.cloned.1.call-start = ((), (), s32[]{:S(2)}) async-start(), calls=%async_computation.1 | async-start | bytes 2162688 | tf_op jit(solution)/shard_map/all_gather | solution.py:21
  7.3 186.1 %all-reduce.2.cloned.1.call-start = ((), (), s32[]{:S(2)}) async-start(), calls=%async_computation.2 | async-start | bytes 7340032 | tf_op jit(solution)/shard_map/psum | solution.py:25
  13.4 6.2 %copy-start.2 = (f32[16,7]{0,1:T(8,128)S(1)}, f32[16,7]{0,1:T(8,128)}, u32[]{:S(2)}) copy-start(f32[16,7]{0,1:T(8,128)} %param.9) | copy-start | bytes 1348
  19.6 0.7 copy-start.3
  20.3 2.0 copy-start
  20.3 3.2 copy-start.1
  87.7 105.6 %copy-start.4 = (f32[7,16]{1,0:T(8,128)S(1)}, f32[7,16]{1,0:T(8,128)}, u32[]{:S(2)}) copy-start(f32[7,16]{1,0:T(8,128)} %param.13) | copy-start | bytes 1348
  87.7 230.6 %reduce-scatter.2.cloned.1.call-start = ((), (), s32[]{:S(2)}) async-start(), calls=%async_computation.3 | async-start | bytes 2162688 | tf_op jit(solution)/shard_map/reduce_scatter | solution.py:27
  193.3 2.0 copy-start.5
  193.3 3.2 copy-start.6
Sparse Core Ops, SparseCore 0:
  9.2 68.8 all-gather.1
  87.9 105.4 all-reduce.1
  202.1 116.1 reduce-scatter.1
where the time goes:
time: 329 us; the launch traced here: 325 us
  waiting for transfers between devices  269 us (82%)
  local copies, waits for them, and re-layouts  19.3 us (6%)
  matrix products  15.1 us (5%)
  between operations  13.1 us (4%)
  other arithmetic  8 us (2%)
    reduce_scatter x1, waiting for transfers between devices, per_device(): lax.psum_scatter(jnp.dot(hidden, down_weight, preferred_element_type=jnp....  116 us
    psum x1, waiting for transfers between devices, per_device(): summed = lax.psum(partial_sums, 'narrow')  105 us
    all_gather x1, waiting for transfers between devices, per_device(): lax.all_gather(tokens, 'wide', axis=0, tiled=True)  46.7 us
    unnamed x16, local copies, waits for them, and re-layouts  17.7 us
    dot_general x1, matrix products, per_device(): jnp.dot(lax.all_gather(tokens, 'wide', axis=0, tiled=True), joined, prefe...  9.57 us
    convert_element_type x1, other arithmetic, dequantize(): (blocks * scale[:, None, :, None]).reshape(height, breadth)  8 us
  transfers between devices with their start and end apart: 3, of which 3 were waited for; matrix products, arithmetic and copies ran while one was open for 7% of the time, Pallas kernels for 0%

commit v1 on v0

v1 whole, which is shorter than its diff:
```python
import functools

import jax
import jax.numpy as jnp
from jax import lax
from jax.experimental import pallas as pl
from jax.experimental.pallas import tpu as pltpu
from jax.sharding import PartitionSpec as P

MESH = pl.DeviceIdType.MESH
BLOCK = 128
TILE = 256
SHARD = 16
OFFSETS = (0, -1, 1, -2, 2, -3, 3, 4)
HALF = 256


def place():
    wide, narrow = lax.axis_index("wide"), lax.axis_index("narrow")
    return wide // 16, (wide // 2) % 8, wide % 2, narrow // 4, narrow % 4


def kernel(
    tokens, gate_codes, gate_scale, up_codes, up_scale, down_codes, down_scale,
    mixed,
    gate_in, up_in, down_in, weight, down, rows, sums, hidden, outs,
    send1, send2, send3, recv1, recv2, recv3,
    core_send, core_recv, side_send, side_recv, ring_send, ring_recv,
    load_sem, a_send, az_recv, ay_recv, ac_recv,
    b_send, b_recv, c_send, c_recv, d_send, d_recv, e_send, e_recv,
):
    y_lo, z, core, y_hi, x = place()
    units = gate_codes.shape[1]
    b1 = ((x + 1) // 2) % 2
    b2 = x // 2
    narrow = y_hi * 4 + x
    wide = y_lo * 16 + z * 2 + core

    def at_z(step):
        return (y_lo * 16 + ((z + step + 8) % 8) * 2 + core, narrow)

    side = ((1 - y_lo) * 16 + z * 2 + core, narrow)
    twin = (y_lo * 16 + z * 2 + 1 - core, narrow)
    first = (wide, y_hi * 4 + x + 1 - 2 * (x % 2))
    second = (wide, y_hi * 4 + 3 - x)
    across = (wide, (1 - y_hi) * 4 + x)

    loads = []
    for index, (source, target) in enumerate(
        ((gate_codes, gate_in), (up_codes, up_in), (down_codes, down_in))
    ):
        loads.append(pltpu.make_async_copy(source, target, load_sem.at[index]))
    own = pltpu.make_async_copy(tokens, rows.at[0, 0, 0, 0], load_sem.at[3])
    own.start()
    for load in loads:
        load.start()

    barrier = pltpu.get_barrier_semaphore()
    partners = [at_z(step) for step in OFFSETS[1:]] + [side, twin, first, second, across]
    for partner in partners:
        pl.semaphore_signal(barrier, inc=1, device_id=partner, device_id_type=MESH)
    pl.semaphore_wait(barrier, len(partners))

    def remote(source, target, send_sem, recv_sem, device):
        copy = pltpu.make_async_remote_copy(
            src_ref=source, dst_ref=target, send_sem=send_sem, recv_sem=recv_sem,
            device_id=device, device_id_type=MESH,
        )
        copy.start()
        return copy

    def shard(slot, other_core, other_side):
        return rows.at[slot // 4, other_core, slot % 4, other_side]

    z_copies, y_copies, c_copies = {}, {}, {}

    def z_send(source, slot, step, columns=None):
        index = slot if columns is None else 7 + columns
        target = shard(slot, 0, 0)
        if columns is not None:
            width = target.shape[1] // 2
            cut = pl.ds(columns * width, width)
            source, target = source.at[:, cut], target.at[:, cut]
        z_copies[index] = remote(source, target, a_send.at[index], az_recv.at[index], at_z(step))

    def y_send(source, slot):
        y_copies[slot] = remote(
            source, shard(slot, 0, 1), a_send.at[9 + slot], ay_recv.at[slot], side
        )

    def c_send_(source, slot, other_side):
        index = slot * 2 + other_side
        c_copies[index] = remote(
            source, shard(slot, 1, other_side), a_send.at[17 + index], ac_recv.at[index], twin
        )

    def spread(slot):
        y_send(shard(slot, 0, 0), slot)
        c_send_(shard(slot, 0, 0), slot, 0)

    def relay(slot):
        y_copies[slot].wait_recv()
        c_send_(shard(slot, 0, 1), slot, 1)

    def widen(step, _):
        span = pl.ds(pl.multiple_of(step * BLOCK, BLOCK), BLOCK)
        for half, (codes, scale) in enumerate(((gate_in, gate_scale), (up_in, up_scale))):
            for col in range(units // BLOCK):
                cut = slice(col * BLOCK, (col + 1) * BLOCK)
                block = codes[span, cut].astype(jnp.float32) * scale[step, col]
                to = slice(half * units + col * BLOCK, half * units + (col + 1) * BLOCK)
                weight[span, to] = block.astype(jnp.bfloat16)
        return 0

    def widen_down(step, _):
        span = pl.ds(pl.multiple_of(step * BLOCK, BLOCK), BLOCK)
        for col in range(down.shape[1] // BLOCK):
            cut = slice(col * BLOCK, (col + 1) * BLOCK)
            block = down_in[span, cut].astype(jnp.float32) * down_scale[step, col]
            down[span, cut] = block.astype(jnp.bfloat16)
        return 0

    z_send(tokens, 1, 1)
    z_send(tokens, 2, -1)
    y_send(tokens, 0)
    c_send_(tokens, 0, 0)
    loads[0].wait()
    loads[1].wait()
    steps = weight.shape[0] // BLOCK
    lax.fori_loop(0, steps // 4, widen, 0)
    z_copies[1].wait_recv()
    z_send(shard(1, 0, 0), 3, 1)
    spread(1)
    z_copies[2].wait_recv()
    z_send(shard(2, 0, 0), 4, -1)
    spread(2)
    relay(0)
    lax.fori_loop(steps // 4, steps // 2, widen, 0)
    z_copies[3].wait_recv()
    z_send(shard(3, 0, 0), 5, 1)
    spread(3)
    z_copies[4].wait_recv()
    z_send(shard(4, 0, 0), 6, -1)
    spread(4)
    relay(1)
    relay(2)
    lax.fori_loop(steps // 2, steps, widen, 0)
    z_copies[5].wait_recv()
    z_send(shard(5, 0, 0), 7, 1, 0)
    spread(5)
    z_copies[6].wait_recv()
    z_send(shard(6, 0, 0), 7, -1, 1)
    spread(6)
    relay(3)

    def multiply(chunk):
        left = rows.at[chunk].reshape(HALF, rows.shape[-1])

        def tile(step, _):
            cut = pl.ds(pl.multiple_of(step * TILE, TILE), TILE)
            sums[pl.ds(chunk * HALF, HALF), cut] = jnp.dot(
                left[...], weight[:, cut], preferred_element_type=jnp.float32
            )
            return 0

        lax.fori_loop(0, weight.shape[1] // TILE, tile, 0)

    lead, follow = (b1, b2), (b2, b1)
    lead_to, follow_to = (first, second), (second, first)
    copies1, copies2, copies3 = {}, {}, {}

    def base(chunk, stream):
        return chunk * HALF + stream * (HALF // 2)

    def span(start, size):
        return pl.ds(pl.multiple_of(start, SHARD), size)

    def scatter1(chunk):
        for stream in range(2):
            at = chunk * 2 + stream
            away = base(chunk, stream) + (1 - lead[stream]) * 64
            send1[at] = sums[span(away, 64), :].astype(jnp.bfloat16)
            copies1[at] = remote(
                send1.at[at], recv1.at[at], b_send.at[at], b_recv.at[at], lead_to[stream]
            )

    def scatter2(chunk):
        for stream in range(2):
            at = chunk * 2 + stream
            copies1[at].wait_recv()
            away = (1 - follow[stream]) * 32
            start = base(chunk, stream) + lead[stream] * 64 + away
            send2[at] = (
                sums[span(start, 32), :] + recv1[at, span(away, 32), :].astype(jnp.float32)
            ).astype(jnp.bfloat16)
            copies2[at] = remote(
                send2.at[at], recv2.at[at], b_send.at[4 + at], b_recv.at[4 + at], follow_to[stream]
            )

    def scatter3(chunk):
        for stream in range(2):
            at = chunk * 2 + stream
            copies2[at].wait_recv()
            away = (1 - y_hi) * SHARD
            inner = follow[stream] * 32 + away
            start = base(chunk, stream) + lead[stream] * 64 + inner
            send3[at] = (
                sums[span(start, SHARD), :]
                + recv1[at, span(inner, SHARD), :].astype(jnp.float32)
                + recv2[at, span(away, SHARD), :].astype(jnp.float32)
            ).astype(jnp.bfloat16)
            copies3[at] = remote(
                send3.at[at], recv3.at[at], b_send.at[8 + at], b_recv.at[8 + at], across
            )

    def mine(chunk, stream):
        return base(chunk, stream) + lead[stream] * 64 + follow[stream] * 32 + y_hi * SHARD

    gathers = {}

    def gather(chunk, stream, stage, start, size, device):
        index = stage * 4 + chunk * 2 + stream
        piece = hidden.at[span(start, size)]
        gathers[stage, chunk, stream] = remote(
            piece, piece, c_send.at[index], c_recv.at[index], device
        )

    def activate(chunk):
        for stream in range(2):
            at = chunk * 2 + stream
            copies3[at].wait_recv()
            inner = follow[stream] * 32 + y_hi * SHARD
            total = (
                sums[span(mine(chunk, stream), SHARD), :]
                + recv1[at, span(inner, SHARD), :].astype(jnp.float32)
                + recv2[at, span(y_hi * SHARD, SHARD), :].astype(jnp.float32)
                + recv3[at].astype(jnp.float32)
            )
            gate, up = total[:, :units], total[:, units:]
            hidden[span(mine(chunk, stream), SHARD), :] = (
                gate / (1.0 + jnp.exp(-gate)) * up
            ).astype(jnp.bfloat16)
            gather(chunk, stream, 0, mine(chunk, stream), SHARD, across)

    def gather2(chunk):
        for stream in range(2):
            gathers[0, chunk, stream].wait_recv()
            start = base(chunk, stream) + lead[stream] * 64 + follow[stream] * 32
            gather(chunk, stream, 1, start, 32, follow_to[stream])

    def gather3(chunk):
        for stream in range(2):
            gathers[1, chunk, stream].wait_recv()
            gather(chunk, stream, 2, base(chunk, stream) + lead[stream] * 64, 64, lead_to[stream])

    twins, sides, rings = {}, {}, {}

    def project(chunk):
        for stream in range(2):
            gathers[2, chunk, stream].wait_recv()

        def tile(step, _):
            cut = pl.ds(pl.multiple_of(step * TILE, TILE), TILE)
            outs[chunk, :, cut] = jnp.dot(
                hidden[pl.ds(chunk * HALF, HALF), :], down[:, cut],
                preferred_element_type=jnp.float32,
            )
            return 0

        lax.fori_loop(0, down.shape[1] // TILE, tile, 0)
        core_send[chunk] = outs[chunk, HALF // 2 :, :].astype(jnp.bfloat16)
        twins[chunk] = remote(
            core_send.at[chunk], core_recv.at[chunk], d_send.at[chunk], d_recv.at[chunk], twin
        )

    def to_side(chunk):
        twins[chunk].wait_recv()
        for slot in range(4):
            away = pl.ds(slot * 32 + SHARD, SHARD)
            side_send[chunk, slot] = (
                outs[chunk, away, :] + core_recv[chunk, away, :].astype(jnp.float32)
            ).astype(jnp.bfloat16)
        sides[chunk] = remote(
            side_send.at[chunk], side_recv.at[chunk],
            d_send.at[2 + chunk], d_recv.at[2 + chunk], side,
        )

    def local(slot):
        chunk, near = slot // 4, pl.ds((slot % 4) * 32, SHARD)
        return (
            outs[chunk, near, :]
            + core_recv[chunk, near, :].astype(jnp.float32)
            + side_recv[chunk, slot % 4].astype(jnp.float32)
        )

    def to_ring(chunk):
        sides[chunk].wait_recv()
        for slot in range(chunk * 4, chunk * 4 + 4):
            if slot > 0:
                ring_send[slot - 1] = local(slot).astype(jnp.bfloat16)
                rings[slot] = remote(
                    ring_send.at[slot - 1], ring_recv.at[slot - 1],
                    e_send.at[slot - 1], e_recv.at[slot - 1], at_z(OFFSETS[slot]),
                )

    own.wait()
    for index in range(8):
        c_copies[index].wait_recv()
    multiply(0)
    scatter1(0)
    z_copies[7].wait_recv()
    z_copies[8].wait_recv()
    spread(7)
    for slot in range(4, 8):
        relay(slot)
    for index in range(8, 16):
        c_copies[index].wait_recv()
    multiply(1)
    scatter1(1)
    loads[2].wait()
    lax.fori_loop(0, down.shape[0] // BLOCK, widen_down, 0)
    scatter2(0)
    scatter3(0)
    scatter2(1)
    activate(0)
    scatter3(1)
    gather2(0)
    activate(1)
    gather3(0)
    gather2(1)
    project(0)
    gather3(1)
    to_side(0)
    to_ring(0)
    project(1)
    to_side(1)
    to_ring(1)
    total = local(0)
    for slot in range(1, 8):
        rings[slot].wait_recv()
        total = total + ring_recv[slot - 1].astype(jnp.float32)
    mixed[...] = total.astype(jnp.bfloat16)

    groups = (z_copies, y_copies, c_copies, copies1, copies2, copies3, gathers, twins, sides, rings)
    for group in groups:
        for copy in group.values():
            copy.wait_send()


def feed_forward(tokens, gate_codes, gate_scale, up_codes, up_scale, down_codes, down_scale):
    depth, units = gate_codes.shape
    bf16, f32 = jnp.bfloat16, jnp.float32
    any_space, scalars = pl.BlockSpec(memory_space=pl.ANY), pl.BlockSpec(memory_space=pltpu.SMEM)
    dma = pltpu.SemaphoreType.DMA
    return pl.pallas_call(
        kernel,
        out_shape=jax.ShapeDtypeStruct(tokens.shape, bf16),
        in_specs=[any_space, any_space, scalars, any_space, scalars, any_space, scalars],
        out_specs=pl.BlockSpec(memory_space=pltpu.VMEM),
        scratch_shapes=[
            pltpu.VMEM((depth, units), bf16),
            pltpu.VMEM((depth, units), bf16),
            pltpu.VMEM((units, depth), bf16),
            pltpu.VMEM((depth, 2 * units), bf16),
            pltpu.VMEM((units, depth), bf16),
            pltpu.VMEM((2, 2, 4, 2, SHARD, depth), bf16),
            pltpu.VMEM((2 * HALF, 2 * units), f32),
            pltpu.VMEM((2 * HALF, units), bf16),
            pltpu.VMEM((2, HALF, depth), f32),
            pltpu.VMEM((4, 64, 2 * units), bf16),
            pltpu.VMEM((4, 32, 2 * units), bf16),
            pltpu.VMEM((4, SHARD, 2 * units), bf16),
            pltpu.VMEM((4, 64, 2 * units), bf16),
            pltpu.VMEM((4, 32, 2 * units), bf16),
            pltpu.VMEM((4, SHARD, 2 * units), bf16),
            pltpu.VMEM((2, HALF // 2, depth), bf16),
            pltpu.VMEM((2, HALF // 2, depth), bf16),
            pltpu.VMEM((2, 4, SHARD, depth), bf16),
            pltpu.VMEM((2, 4, SHARD, depth), bf16),
            pltpu.VMEM((7, SHARD, depth), bf16),
            pltpu.VMEM((7, SHARD, depth), bf16),
            dma((4,)),
            dma((33,)),
            dma((9,)),
            dma((8,)),
            dma((16,)),
            dma((12,)),
            dma((12,)),
            dma((12,)),
            dma((12,)),
            dma((4,)),
            dma((4,)),
            dma((7,)),
            dma((7,)),
        ],
        compiler_params=pltpu.CompilerParams(
            collective_id=0, has_side_effects=True, vmem_limit_bytes=56 << 20
        ),
    )(tokens, gate_codes, gate_scale, up_codes, up_scale, down_codes, down_scale)


def solution(mesh):
    return jax.shard_map(
        feed_forward,
        mesh=mesh,
        in_specs=(
            P("wide", "narrow"),
            P("narrow", "wide"),
            P("narrow", "wide"),
            P("narrow", "wide"),
            P("narrow", "wide"),
            P("wide", "narrow"),
            P("wide", "narrow"),
        ),
        out_specs=P("wide", "narrow"),
        check_vma=False,
    )
```

time: 329 us -> 99.2 us (0.30); the launches traced: 325 us -> 98.5 us
  waiting for transfers between devices: 269 us -> 0 us
  Pallas kernels: 0 us -> 94.3 us
  local copies, waits for them, and re-layouts: 19.3 us -> 4.19 us
  matrix products: 15.1 us -> 0 us
  between operations: 13.1 us -> 0.01 us
  other arithmetic: 8 us -> 0 us
    reduce_scatter x1 -> x0, waiting for transfers between devices: 116 us -> none  [per_device(): lax.psum_scatter(jnp.dot(hidden, down_weight, preferred_element_type=jnp....]
    psum x1 -> x0, waiting for transfers between devices: 105 us -> none  [per_device(): summed = lax.psum(partial_sums, 'narrow')]
    pallas_call x0 -> x1, Pallas kernels: none -> 94.3 us  [feed_forward(): pl.pallas_call(kernel, out_shape=jax.ShapeDtypeStruct(tokens.shape, bf16)...]
    all_gather x1 -> x0, waiting for transfers between devices: 46.7 us -> none  [per_device(): lax.all_gather(tokens, 'wide', axis=0, tiled=True)]
    dot_general x2 -> x0, matrix products: 15.1 us -> none  [the longest x1 9.57 us: per_device(): jnp.dot(lax.all_gather(tokens, 'wide', axis=0, tiled=True), joined, prefe...]
    unnamed x16 -> x3, local copies, waits for them, and re-layouts: 17.7 us -> 4.19 us
    convert_element_type x1 -> x0, other arithmetic: 8 us -> none  [dequantize(): (blocks * scale[:, None, :, None]).reshape(height, breadth)]
  transfers between devices with their start and end apart: 3 -> 0, of which waited for: 3 -> 0; matrix products, arithmetic and copies ran while one was open for 7% -> 0% of each run, Pallas kernels for 0% -> 0%
where the time goes in v1:
time: 99.2 us; the launch traced here: 98.5 us
  Pallas kernels  94.3 us (95%)
  local copies, waits for them, and re-layouts  4.19 us (4%)
    pallas_call x1, Pallas kernels, feed_forward(): pl.pallas_call(kernel, out_shape=jax.ShapeDtypeStruct(tokens.shape, bf16)...  94.3 us
    unnamed x3, local copies, waits for them, and re-layouts  4.19 us

profile of v1, /device:TPU:1, one launch (start us, length us, event | category | flops | bytes accessed | tf_op | source)
XLA Modules:
  0.0 98.5 jit_solution(12886945522323776428)
XLA Ops:
  0.0 1.4 %copy.8.gate_scale = f32[16,7]{1,0:T(8,128)} copy(f32[16,7]{0,1:T(8,128)} %param.9) | data formatting | bytes 896 | tf_op args[2]
  1.4 1.4 %copy.9.up_scale = f32[16,7]{1,0:T(8,128)} copy(f32[16,7]{0,1:T(8,128)} %param.11) | data formatting | bytes 896 | tf_op args[4]
  2.7 94.3 %shard_map.73 = bf16[16,2048]{1,0:T(8,128)(2,1)} custom-call(bf16[16,2048]{1,0:T(8,128)(2,1)} %tokens.1, bf16[2048,896]{1,0:T(8,128)(2,1)} %gate_codes.1, f32[16,7]{1,0:T(8,128)} %copy.8.gate_scale, bf16[2048,896]{1,0:T(8,128)(2,1)} %up_codes.1, f32[16,7]{1,0:T(8,128)} %copy.9.up_scale, bf16[896,2048]{1,0:T(8,128)(2,1)} %down_codes.1, f32[7,16]{1,0:T(8,128)} %down_scale.1), custom_call_target="tpu_custom_call" | custom-call | tf_op jit(solution)/shard_map/pallas_call | solution.py:355
  97.0 1.5 %copy.11 = bf16[16,2048]{1,0:T(8,128)(2,1)} copy(bf16[16,2048]{1,0:T(8,128)(2,1)} %shard_map.73) | data formatting | bytes 131072

commit v2 on v0

v2 whole, which is shorter than its diff:
```python
import jax
import jax.numpy as jnp
from jax import lax
from jax.experimental import pallas as pl
from jax.experimental.pallas import tpu as pltpu
from jax.sharding import PartitionSpec as P

MESH = pl.DeviceIdType.MESH
BLOCK = 128
TILE = 256
SHARD = 16
UNITS = 4
UNIT = 128
QUARTER = 64
COPIES = 128
OFFSETS = (1, -1, 3, -3, 4, 0, 2, -2)


def kernel(
    tokens, gate_codes, gate_scale, up_codes, up_scale, down_codes, down_scale,
    mixed,
    gate_in, up_in, down_in, weight, down, rows, sums, hidden, outs,
    send1, send2, recv1, recv2,
    core_send, core_recv, side_send, side_recv, ring_send, ring_recv, last_send, last_recv,
    load_sem, send_sem, recv_sem,
):
    wide, narrow = lax.axis_index("wide"), lax.axis_index("narrow")
    y_lo, z, core, y_hi, x = wide // 16, (wide // 2) % 8, wide % 2, narrow // 4, narrow % 4
    units = gate_codes.shape[1]

    def at_z(step, other_side=0):
        y = 1 - y_lo if other_side else y_lo
        return (y * 16 + ((z + step + 8) % 8) * 2 + core, narrow)

    side = ((1 - y_lo) * 16 + z * 2 + core, narrow)
    twin = (y_lo * 16 + z * 2 + 1 - core, narrow)
    first_x, second_x = x + 1 - 2 * (x % 2), 3 - x
    bits = (((x + 1) // 2) % 2, x // 2)
    pairs = ((wide, y_hi * 4 + first_x), (wide, y_hi * 4 + second_x))
    across = (wide, (1 - y_hi) * 4 + x)
    diagonals = ((wide, (1 - y_hi) * 4 + first_x), (wide, (1 - y_hi) * 4 + second_x))

    loads = [
        pltpu.make_async_copy(source, target, load_sem.at[index])
        for index, (source, target) in enumerate(
            (
                (tokens, rows.at[OFFSETS.index(0) // 2, 0, OFFSETS.index(0) % 2, 0]),
                (gate_codes, gate_in),
                (up_codes, up_in),
                (down_codes, down_in),
            )
        )
    ]
    for load in loads:
        load.start()

    barrier = pltpu.get_barrier_semaphore()
    partners = [at_z(step) for step in OFFSETS if step] + [at_z(2, 1), at_z(-2, 1)]
    partners += [side, twin, across, *pairs, *diagonals]
    for partner in partners:
        pl.semaphore_signal(barrier, inc=1, device_id=partner, device_id_type=MESH)
    pl.semaphore_wait(barrier, len(partners))

    started = []

    def remote(source, target, device):
        index = len(started)
        copy = pltpu.make_async_remote_copy(
            src_ref=source, dst_ref=target,
            send_sem=send_sem.at[index], recv_sem=recv_sem.at[index],
            device_id=device, device_id_type=MESH,
        )
        copy.start()
        started.append(copy)
        return copy

    def shard(offset, other_core, other_side):
        slot = OFFSETS.index(offset)
        return rows.at[slot // 2, other_core, slot % 2, other_side]

    arrivals = {}

    def to_twin(offset, other_side):
        arrivals[offset, 1, other_side] = remote(
            shard(offset, 0, other_side), shard(offset, 1, other_side), twin
        )

    def to_other_side(offset):
        arrivals[offset, 0, 1] = [remote(shard(offset, 0, 0), shard(offset, 0, 1), side)]

    def take(offset, other_side):
        for copy in arrivals[offset, 0, other_side]:
            copy.wait_recv()
        to_twin(offset, other_side)

    middle = BLOCK * ((units // BLOCK + 1) // 2)
    streams = ((0, middle), (middle, units))

    def both(stream):
        start, end = streams[stream]
        return pl.ds(2 * start, 2 * (end - start))

    def widen(step, _):
        span = pl.ds(pl.multiple_of(step * BLOCK, BLOCK), BLOCK)
        for second, (codes, scale) in enumerate(((gate_in, gate_scale), (up_in, up_scale))):
            for start, end in streams:
                for at in range(start, end, BLOCK):
                    block = codes[span, at : at + BLOCK].astype(jnp.float32) * scale[at // BLOCK, step]
                    to = start + at + second * (end - start)
                    weight[span, to : to + BLOCK] = block.astype(jnp.bfloat16)
        return 0

    def widen_down(step, _):
        span = pl.ds(pl.multiple_of(step * BLOCK, BLOCK), BLOCK)
        for col in range(down.shape[1] // BLOCK):
            cut = slice(col * BLOCK, (col + 1) * BLOCK)
            block = down_in[span, cut].astype(jnp.float32) * down_scale[step, col]
            down[span, cut] = block.astype(jnp.bfloat16)
        return 0

    def span(start, size):
        return pl.ds(pl.multiple_of(start, SHARD), size)

    def lead(unit, stream):
        return (unit + stream) % 2

    def base(unit, stream):
        return unit * UNIT + bits[lead(unit, stream)] * QUARTER

    def within(unit, stream, other_x, other_y):
        follow = bits[1 - lead(unit, stream)]
        return (1 - follow if other_x else follow) * 32 + (1 - y_hi if other_y else y_hi) * SHARD

    def trio(unit, stream):
        follow = 1 - lead(unit, stream)
        return ((1, 0, pairs[follow]), (0, 1, across), (1, 1, diagonals[follow]))

    halves, quarters, gathers, forwards = {}, {}, {}, {}

    def multiply(unit):
        for offset in OFFSETS[2 * unit : 2 * unit + 2]:
            arrivals[offset, 1, 0].wait_recv()
            arrivals[offset, 1, 1].wait_recv()

        def tile(step, _):
            cut = pl.ds(pl.multiple_of(step * TILE, TILE), TILE)
            left = rows[unit].reshape(UNIT, rows.shape[-1])
            sums[pl.ds(unit * UNIT, UNIT), cut] = jnp.dot(
                left, weight[:, cut], preferred_element_type=jnp.float32
            )
            return 0

        for stream, (start, end) in enumerate(streams):
            lax.fori_loop(2 * start // TILE, 2 * end // TILE, tile, 0)
            away = unit * UNIT + (1 - bits[lead(unit, stream)]) * QUARTER
            cut = both(stream)
            send1[unit, :, cut] = sums[span(away, QUARTER), cut].astype(jnp.bfloat16)
            halves[unit, stream] = remote(
                send1.at[unit, :, cut], recv1.at[unit, :, cut], pairs[lead(unit, stream)]
            )

    def partial(unit, stream, other_x, other_y):
        inner, cut = within(unit, stream, other_x, other_y), both(stream)
        return sums[span(base(unit, stream) + inner, SHARD), cut] + recv1[
            unit, span(inner, SHARD), cut
        ].astype(jnp.float32)

    def scatter(unit):
        for stream in range(2):
            halves[unit, stream].wait_recv()
            cut = both(stream)
            for index, (other_x, other_y, device) in enumerate(trio(unit, stream)):
                send2[unit, index, :, cut] = partial(unit, stream, other_x, other_y).astype(
                    jnp.bfloat16
                )
                quarters[unit, stream, index] = remote(
                    send2.at[unit, index, :, cut], recv2.at[unit, index, :, cut], device
                )

    def activate(unit):
        for stream, (start, end) in enumerate(streams):
            total = partial(unit, stream, 0, 0)
            for index in range(3):
                quarters[unit, stream, index].wait_recv()
                total = total + recv2[unit, index, :, both(stream)].astype(jnp.float32)
            gate, up = total[:, : end - start], total[:, end - start :]
            mine = span(base(unit, stream) + within(unit, stream, 0, 0), SHARD)
            hidden[mine, start:end] = (gate / (1.0 + jnp.exp(-gate)) * up).astype(jnp.bfloat16)
            piece = hidden.at[mine, pl.ds(start, end - start)]
            for index, (_, _, device) in enumerate(trio(unit, stream)):
                gathers[unit, stream, index] = remote(piece, piece, device)

    def forward(unit):
        for stream, (start, end) in enumerate(streams):
            for index in range(3):
                gathers[unit, stream, index].wait_recv()
            piece = hidden.at[span(base(unit, stream), QUARTER), pl.ds(start, end - start)]
            forwards[unit, stream] = remote(piece, piece, pairs[lead(unit, stream)])

    twins, sides, rings, lasts, folded = {}, {}, {}, {}, []

    def project(unit):
        for stream in range(2):
            forwards[unit, stream].wait_recv()

        def tile(step, _):
            cut = pl.ds(pl.multiple_of(step * TILE, TILE), TILE)
            outs[unit, :, cut] = jnp.dot(
                hidden[pl.ds(unit * UNIT, UNIT), :], down[:, cut],
                preferred_element_type=jnp.float32,
            )
            return 0

        lax.fori_loop(0, down.shape[1] // TILE, tile, 0)
        core_send[unit] = outs[unit, QUARTER:, :].astype(jnp.bfloat16)
        twins[unit] = remote(core_send.at[unit], core_recv.at[unit], twin)

    def paired(slot, other_side):
        at = pl.ds((slot % 2) * 32 + other_side * SHARD, SHARD)
        return outs[slot // 2, at, :] + core_recv[slot // 2, at, :].astype(jnp.float32)

    def to_side(unit):
        twins[unit].wait_recv()
        for slot in (2 * unit, 2 * unit + 1):
            side_send[slot] = paired(slot, 1).astype(jnp.bfloat16)
        cut = pl.ds(2 * unit, 2)
        sides[unit] = remote(side_send.at[cut], side_recv.at[cut], side)

    def local(slot):
        return paired(slot, 0) + side_recv[slot].astype(jnp.float32)

    def to_ring(unit):
        sides[unit].wait_recv()
        for slot in (2 * unit, 2 * unit + 1):
            folded.append(slot)
            if OFFSETS[slot]:
                ring_send[slot] = local(slot).astype(jnp.bfloat16)
                rings[slot] = remote(ring_send.at[slot], ring_recv.at[slot], at_z(OFFSETS[slot]))

    def straight(unit):
        twins[unit].wait_recv()
        for slot in (2 * unit, 2 * unit + 1):
            for other_side in range(2):
                if OFFSETS[slot] or other_side:
                    index = (slot % 2) * 2 + other_side
                    last_send[index] = paired(slot, other_side).astype(jnp.bfloat16)
                    lasts[index] = remote(
                        last_send.at[index], last_recv.at[index], at_z(OFFSETS[slot], other_side)
                    )

    loads[0].wait()
    for offset in (1, -1):
        arrivals[offset, 0, 0] = [remote(shard(0, 0, 0), shard(offset, 0, 0), at_z(-offset))]
    to_other_side(0)
    for offset in (2, -2):
        arrivals[offset, 0, 0] = [remote(shard(0, 0, 0), shard(offset, 0, 0), at_z(-offset))]
    to_twin(0, 0)
    arrivals[4, 0, 0] = []
    steps = weight.shape[0] // BLOCK
    loads[1].wait()
    loads[2].wait()
    lax.fori_loop(0, steps // 4, widen, 0)
    take(0, 1)
    for offset in (1, -1):
        arrivals[offset, 0, 1] = [remote(shard(0, 0, 1), shard(offset, 0, 1), at_z(-offset))]
    take(1, 0)
    take(-1, 0)
    lax.fori_loop(steps // 4, steps // 2, widen, 0)
    half = tokens.shape[1] // 2
    for offset, sign, columns in ((2, 1, pl.ds(0, half)), (-2, -1, pl.ds(half, half))):
        take(offset, 0)
        here = shard(offset, 0, 0)
        arrivals[3 * sign, 0, 0] = [remote(here, shard(3 * sign, 0, 0), at_z(-sign))]
        arrivals[4, 0, 0].append(
            remote(here.at[:, columns], shard(4, 0, 0).at[:, columns], at_z(-2 * sign))
        )
        to_other_side(offset)
    lax.fori_loop(steps // 2, steps, widen, 0)
    take(1, 1)
    take(-1, 1)
    multiply(0)
    take(3, 0)
    to_other_side(3)
    take(2, 1)
    take(-3, 0)
    to_other_side(-3)
    take(-2, 1)
    take(4, 0)
    to_other_side(4)
    multiply(3)
    take(3, 1)
    take(-3, 1)
    loads[3].wait()
    lax.fori_loop(0, down.shape[0] // BLOCK, widen_down, 0)
    scatter(0)
    multiply(1)
    take(4, 1)
    scatter(3)
    multiply(2)
    activate(0)
    scatter(1)
    activate(3)
    scatter(2)
    forward(0)
    activate(1)
    forward(3)
    project(0)
    activate(2)
    to_side(0)
    forward(1)
    project(3)
    to_side(3)
    forward(2)
    project(1)
    to_ring(0)
    to_side(1)
    project(2)
    to_ring(3)
    to_side(2)
    to_ring(1)
    to_ring(2)
    total = paired(OFFSETS.index(0), 0)
    if OFFSETS.index(0) in folded:
        total = local(OFFSETS.index(0))
    for slot, copy in rings.items():
        copy.wait_recv()
        total = total + ring_recv[slot].astype(jnp.float32)
    for index, copy in lasts.items():
        copy.wait_recv()
        total = total + last_recv[index].astype(jnp.float32)
    mixed[...] = total.astype(jnp.bfloat16)

    for copy in started:
        copy.wait_send()


def feed_forward(tokens, gate_codes, gate_scale, up_codes, up_scale, down_codes, down_scale):
    depth, units = gate_codes.shape
    bf16, f32 = jnp.bfloat16, jnp.float32
    any_space, scalars = pl.BlockSpec(memory_space=pl.ANY), pl.BlockSpec(memory_space=pltpu.SMEM)
    dma = pltpu.SemaphoreType.DMA
    return pl.pallas_call(
        kernel,
        out_shape=jax.ShapeDtypeStruct(tokens.shape, bf16),
        in_specs=[any_space, any_space, scalars, any_space, scalars, any_space, scalars],
        out_specs=pl.BlockSpec(memory_space=pltpu.VMEM),
        scratch_shapes=[
            pltpu.VMEM((depth, units), bf16),
            pltpu.VMEM((depth, units), bf16),
            pltpu.VMEM((units, depth), bf16),
            pltpu.VMEM((depth, 2 * units), bf16),
            pltpu.VMEM((units, depth), bf16),
            pltpu.VMEM((UNITS, 2, 2, 2, SHARD, depth), bf16),
            pltpu.VMEM((UNITS * UNIT, 2 * units), f32),
            pltpu.VMEM((UNITS * UNIT, units), bf16),
            pltpu.VMEM((UNITS, UNIT, depth), f32),
            pltpu.VMEM((UNITS, QUARTER, 2 * units), bf16),
            pltpu.VMEM((UNITS, 3, SHARD, 2 * units), bf16),
            pltpu.VMEM((UNITS, QUARTER, 2 * units), bf16),
            pltpu.VMEM((UNITS, 3, SHARD, 2 * units), bf16),
            pltpu.VMEM((UNITS, QUARTER, depth), bf16),
            pltpu.VMEM((UNITS, QUARTER, depth), bf16),
            pltpu.VMEM((2 * UNITS, SHARD, depth), bf16),
            pltpu.VMEM((2 * UNITS, SHARD, depth), bf16),
            pltpu.VMEM((2 * UNITS, SHARD, depth), bf16),
            pltpu.VMEM((2 * UNITS, SHARD, depth), bf16),
            pltpu.VMEM((4, SHARD, depth), bf16),
            pltpu.VMEM((4, SHARD, depth), bf16),
            dma((4,)),
            dma((COPIES,)),
            dma((COPIES,)),
        ],
        compiler_params=pltpu.CompilerParams(
            collective_id=0, has_side_effects=True, vmem_limit_bytes=56 << 20
        ),
    )(tokens, gate_codes, gate_scale.T, up_codes, up_scale.T, down_codes, down_scale)


def solution(mesh):
    return jax.shard_map(
        feed_forward,
        mesh=mesh,
        in_specs=(
            P("wide", "narrow"),
            P("narrow", "wide"),
            P("narrow", "wide"),
            P("narrow", "wide"),
            P("narrow", "wide"),
            P("wide", "narrow"),
            P("wide", "narrow"),
        ),
        out_specs=P("wide", "narrow"),
        check_vma=False,
    )
```

time: 329 us -> 75 us (0.23); the launches traced: 325 us -> 74.3 us
  waiting for transfers between devices: 269 us -> 0 us
  Pallas kernels: 0 us -> 72.8 us
  local copies, waits for them, and re-layouts: 19.3 us -> 1.47 us
  matrix products: 15.1 us -> 0 us
  between operations: 13.1 us -> 0.01 us
  other arithmetic: 8 us -> 0 us
    reduce_scatter x1 -> x0, waiting for transfers between devices: 116 us -> none  [per_device(): lax.psum_scatter(jnp.dot(hidden, down_weight, preferred_element_type=jnp....]
    psum x1 -> x0, waiting for transfers between devices: 105 us -> none  [per_device(): summed = lax.psum(partial_sums, 'narrow')]
    pallas_call x0 -> x1, Pallas kernels: none -> 72.8 us  [feed_forward(): pl.pallas_call(kernel, out_shape=jax.ShapeDtypeStruct(tokens.shape, bf16)...]
    all_gather x1 -> x0, waiting for transfers between devices: 46.7 us -> none  [per_device(): lax.all_gather(tokens, 'wide', axis=0, tiled=True)]
    unnamed x16 -> x1, local copies, waits for them, and re-layouts: 17.7 us -> 1.47 us
    dot_general x2 -> x0, matrix products: 15.1 us -> none  [the longest x1 9.57 us: per_device(): jnp.dot(lax.all_gather(tokens, 'wide', axis=0, tiled=True), joined, prefe...]
    convert_element_type x1 -> x0, other arithmetic: 8 us -> none  [dequantize(): (blocks * scale[:, None, :, None]).reshape(height, breadth)]
  transfers between devices with their start and end apart: 3 -> 0, of which waited for: 3 -> 0; matrix products, arithmetic and copies ran while one was open for 7% -> 0% of each run, Pallas kernels for 0% -> 0%
where the time goes in v2:
time: 75 us; the launch traced here: 74.3 us
  Pallas kernels  72.8 us (97%)
  local copies, waits for them, and re-layouts  1.47 us (2%)
    pallas_call x1, Pallas kernels, feed_forward(): pl.pallas_call(kernel, out_shape=jax.ShapeDtypeStruct(tokens.shape, bf16)...  72.8 us

profile of v2, /device:TPU:1, one launch (start us, length us, event | category | flops | bytes accessed | tf_op | source)
XLA Modules:
  0.0 74.3 jit_solution(14013384742485062246)
XLA Ops:
  0.0 72.8 %shard_map.73 = bf16[16,2048]{1,0:T(8,128)(2,1)} custom-call(bf16[16,2048]{1,0:T(8,128)(2,1)} %tokens.1, bf16[2048,896]{1,0:T(8,128)(2,1)} %gate_codes.1, f32[7,16]{1,0:T(8,128)} %bitcast.2, bf16[2048,896]{1,0:T(8,128)(2,1)} %up_codes.1, f32[7,16]{1,0:T(8,128)} %bitcast.3, bf16[896,2048]{1,0:T(8,128)(2,1)} %down_codes.1, f32[7,16]{1,0:T(8,128)} %down_scale.1), custom_call_target="tpu_custom_call" | custom-call | tf_op jit(solution)/shard_map/pallas_call | solution.py:342
  72.8 1.5 %copy.9 = bf16[16,2048]{1,0:T(8,128)(2,1)} copy(bf16[16,2048]{1,0:T(8,128)(2,1)} %shard_map.73) | data formatting | bytes 131072

commit v3 on v2

--- a/solution.py
+++ b/solution.py
@@ -7,7 +7,6 @@
 
 MESH = pl.DeviceIdType.MESH
 BLOCK = 128
-TILE = 256
 SHARD = 16
 UNITS = 4
 UNIT = 128
@@ -21,16 +20,15 @@
     mixed,
     gate_in, up_in, down_in, weight, down, rows, sums, hidden, outs,
     send1, send2, recv1, recv2,
-    core_send, core_recv, side_send, side_recv, ring_send, ring_recv, last_send, last_recv,
+    core_send, core_recv, side_send, side_recv, ring_send, ring_recv,
     load_sem, send_sem, recv_sem,
 ):
     wide, narrow = lax.axis_index("wide"), lax.axis_index("narrow")
     y_lo, z, core, y_hi, x = wide // 16, (wide // 2) % 8, wide % 2, narrow // 4, narrow % 4
     units = gate_codes.shape[1]
 
-    def at_z(step, other_side=0):
-        y = 1 - y_lo if other_side else y_lo
-        return (y * 16 + ((z + step + 8) % 8) * 2 + core, narrow)
+    def at_z(step):
+        return (y_lo * 16 + ((z + step + 8) % 8) * 2 + core, narrow)
 
     side = ((1 - y_lo) * 16 + z * 2 + core, narrow)
     twin = (y_lo * 16 + z * 2 + 1 - core, narrow)
@@ -55,7 +53,7 @@
         load.start()
 
     barrier = pltpu.get_barrier_semaphore()
-    partners = [at_z(step) for step in OFFSETS if step] + [at_z(2, 1), at_z(-2, 1)]
+    partners = [at_z(step) for step in OFFSETS if step]
     partners += [side, twin, across, *pairs, *diagonals]
     for partner in partners:
         pl.semaphore_signal(barrier, inc=1, device_id=partner, device_id_type=MESH)
@@ -142,18 +140,13 @@
             arrivals[offset, 1, 0].wait_recv()
             arrivals[offset, 1, 1].wait_recv()
 
-        def tile(step, _):
-            cut = pl.ds(pl.multiple_of(step * TILE, TILE), TILE)
-            left = rows[unit].reshape(UNIT, rows.shape[-1])
+        for stream in range(2):
+            cut = both(stream)
             sums[pl.ds(unit * UNIT, UNIT), cut] = jnp.dot(
-                left, weight[:, cut], preferred_element_type=jnp.float32
-            )
-            return 0
-
-        for stream, (start, end) in enumerate(streams):
-            lax.fori_loop(2 * start // TILE, 2 * end // TILE, tile, 0)
+                rows[unit].reshape(UNIT, rows.shape[-1]), weight[:, cut],
+                preferred_element_type=jnp.float32,
+            )
             away = unit * UNIT + (1 - bits[lead(unit, stream)]) * QUARTER
-            cut = both(stream)
             send1[unit, :, cut] = sums[span(away, QUARTER), cut].astype(jnp.bfloat16)
             halves[unit, stream] = remote(
                 send1.at[unit, :, cut], recv1.at[unit, :, cut], pairs[lead(unit, stream)]
@@ -197,30 +190,32 @@
             piece = hidden.at[span(base(unit, stream), QUARTER), pl.ds(start, end - start)]
             forwards[unit, stream] = remote(piece, piece, pairs[lead(unit, stream)])
 
-    twins, sides, rings, lasts, folded = {}, {}, {}, {}, []
+    twins, sides, rings = {}, {}, {}
 
     def project(unit):
         for stream in range(2):
             forwards[unit, stream].wait_recv()
 
-        def tile(step, _):
-            cut = pl.ds(pl.multiple_of(step * TILE, TILE), TILE)
+        half = down.shape[1] // 2
+        twins[unit] = []
+        for part in range(2):
+            cut = pl.ds(part * half, half)
             outs[unit, :, cut] = jnp.dot(
                 hidden[pl.ds(unit * UNIT, UNIT), :], down[:, cut],
                 preferred_element_type=jnp.float32,
             )
-            return 0
-
-        lax.fori_loop(0, down.shape[1] // TILE, tile, 0)
-        core_send[unit] = outs[unit, QUARTER:, :].astype(jnp.bfloat16)
-        twins[unit] = remote(core_send.at[unit], core_recv.at[unit], twin)
+            core_send[unit, :, cut] = outs[unit, QUARTER:, cut].astype(jnp.bfloat16)
+            twins[unit].append(
+                remote(core_send.at[unit, :, cut], core_recv.at[unit, :, cut], twin)
+            )
 
     def paired(slot, other_side):
         at = pl.ds((slot % 2) * 32 + other_side * SHARD, SHARD)
         return outs[slot // 2, at, :] + core_recv[slot // 2, at, :].astype(jnp.float32)
 
     def to_side(unit):
-        twins[unit].wait_recv()
+        for copy in twins[unit]:
+            copy.wait_recv()
         for slot in (2 * unit, 2 * unit + 1):
             side_send[slot] = paired(slot, 1).astype(jnp.bfloat16)
         cut = pl.ds(2 * unit, 2)
@@ -232,21 +227,9 @@
     def to_ring(unit):
         sides[unit].wait_recv()
         for slot in (2 * unit, 2 * unit + 1):
-            folded.append(slot)
             if OFFSETS[slot]:
                 ring_send[slot] = local(slot).astype(jnp.bfloat16)
                 rings[slot] = remote(ring_send.at[slot], ring_recv.at[slot], at_z(OFFSETS[slot]))
-
-    def straight(unit):
-        twins[unit].wait_recv()
-        for slot in (2 * unit, 2 * unit + 1):
-            for other_side in range(2):
-                if OFFSETS[slot] or other_side:
-                    index = (slot % 2) * 2 + other_side
-                    last_send[index] = paired(slot, other_side).astype(jnp.bfloat16)
-                    lasts[index] = remote(
-                        last_send.at[index], last_recv.at[index], at_z(OFFSETS[slot], other_side)
-                    )
 
     loads[0].wait()
     for offset in (1, -1):
@@ -319,15 +302,10 @@
     to_side(2)
     to_ring(1)
     to_ring(2)
-    total = paired(OFFSETS.index(0), 0)
-    if OFFSETS.index(0) in folded:
-        total = local(OFFSETS.index(0))
+    total = local(OFFSETS.index(0))
     for slot, copy in rings.items():
         copy.wait_recv()
         total = total + ring_recv[slot].astype(jnp.float32)
-    for index, copy in lasts.items():
-        copy.wait_recv()
-        total = total + last_recv[index].astype(jnp.float32)
     mixed[...] = total.astype(jnp.bfloat16)
 
     for copy in started:
@@ -341,7 +319,7 @@
     dma = pltpu.SemaphoreType.DMA
     return pl.pallas_call(
         kernel,
-        out_shape=jax.ShapeDtypeStruct(tokens.shape, bf16),
+        out_shape=pltpu.VMEM(tokens.shape, bf16),
         in_specs=[any_space, any_space, scalars, any_space, scalars, any_space, scalars],
         out_specs=pl.BlockSpec(memory_space=pltpu.VMEM),
         scratch_shapes=[
@@ -364,8 +342,6 @@
             pltpu.VMEM((2 * UNITS, SHARD, depth), bf16),
             pltpu.VMEM((2 * UNITS, SHARD, depth), bf16),
             pltpu.VMEM((2 * UNITS, SHARD, depth), bf16),
-            pltpu.VMEM((4, SHARD, depth), bf16),
-            pltpu.VMEM((4, SHARD, depth), bf16),
             dma((4,)),
             dma((COPIES,)),
             dma((COPIES,)),

time: 75 us -> 71.3 us (0.951)
  Pallas kernels: 72.8 us -> 70.6 us
  local copies, waits for them, and re-layouts: 1.47 us -> 0.63 us
    pallas_call x1, Pallas kernels: 72.8 us -> 70.6 us  [feed_forward(): pl.pallas_call(kernel, out_shape=pltpu.VMEM(tokens.shape, bf16), in_specs...]
    unnamed x1, local copies, waits for them, and re-layouts: 1.47 us -> 0.63 us
where the time goes in v3:
time: 71.3 us; the launch traced here: 71.2 us
  Pallas kernels  70.6 us (99%)
    pallas_call x1, Pallas kernels, feed_forward(): pl.pallas_call(kernel, out_shape=pltpu.VMEM(tokens.shape, bf16), in_specs...  70.6 us

profile of v3, /device:TPU:1, one launch (start us, length us, event | category | flops | bytes accessed | tf_op | source)
XLA Modules:
  0.0 71.2 jit_solution(17778124844647560236)
XLA Ops:
  0.0 70.6 %shard_map.73 = bf16[16,2048]{1,0:T(8,128)(2,1)S(1)} custom-call(bf16[16,2048]{1,0:T(8,128)(2,1)} %tokens.1, bf16[2048,896]{1,0:T(8,128)(2,1)} %gate_codes.1, f32[7,16]{1,0:T(8,128)} %bitcast.2, bf16[2048,896]{1,0:T(8,128)(2,1)} %up_codes.1, f32[7,16]{1,0:T(8,128)} %bitcast.3, bf16[896,2048]{1,0:T(8,128)(2,1)} %down_codes.1, f32[7,16]{1,0:T(8,128)} %down_scale.1), custom_call_target="tpu_custom_call" | custom-call | tf_op jit(solution)/shard_map/pallas_call | solution.py:320
  70.6 0.6 copy.9

commit v4 on v3

--- a/solution.py
+++ b/solution.py
@@ -12,7 +12,7 @@
 UNIT = 128
 QUARTER = 64
 COPIES = 128
-OFFSETS = (1, -1, 3, -3, 4, 0, 2, -2)
+OFFSETS = (1, -1, 2, -2, 3, -3, 4, 0)
 
 
 def kernel(
@@ -53,7 +53,7 @@
         load.start()
 
     barrier = pltpu.get_barrier_semaphore()
-    partners = [at_z(step) for step in OFFSETS if step]
+    partners = [at_z(step) for step in (1, -1, 2, -2)]
     partners += [side, twin, across, *pairs, *diagonals]
     for partner in partners:
         pl.semaphore_signal(barrier, inc=1, device_id=partner, device_id_type=MESH)
@@ -262,46 +262,46 @@
     take(1, 1)
     take(-1, 1)
     multiply(0)
+    take(-3, 0)
+    to_other_side(-3)
+    take(-2, 1)
     take(3, 0)
     to_other_side(3)
     take(2, 1)
-    take(-3, 0)
-    to_other_side(-3)
-    take(-2, 1)
+    multiply(1)
+    take(-3, 1)
     take(4, 0)
     to_other_side(4)
-    multiply(3)
-    take(3, 1)
-    take(-3, 1)
     loads[3].wait()
     lax.fori_loop(0, down.shape[0] // BLOCK, widen_down, 0)
     scatter(0)
-    multiply(1)
+    take(3, 1)
+    multiply(2)
     take(4, 1)
+    scatter(1)
+    multiply(3)
+    activate(0)
+    scatter(2)
+    activate(1)
     scatter(3)
-    multiply(2)
-    activate(0)
-    scatter(1)
+    forward(0)
+    activate(2)
+    forward(1)
+    project(0)
     activate(3)
-    scatter(2)
-    forward(0)
-    activate(1)
-    forward(3)
-    project(0)
-    activate(2)
     to_side(0)
-    forward(1)
-    project(3)
-    to_side(3)
     forward(2)
     project(1)
+    to_side(1)
+    forward(3)
+    project(2)
     to_ring(0)
-    to_side(1)
-    project(2)
+    to_side(2)
+    project(3)
+    to_ring(1)
+    to_side(3)
+    to_ring(2)
     to_ring(3)
-    to_side(2)
-    to_ring(1)
-    to_ring(2)
     total = local(OFFSETS.index(0))
     for slot, copy in rings.items():
         copy.wait_recv()

time: 71.3 us -> 70 us (0.982)
  Pallas kernels: 70.6 us -> 69.3 us
    pallas_call x1, Pallas kernels: 70.6 us -> 69.3 us  [feed_forward(): pl.pallas_call(kernel, out_shape=pltpu.VMEM(tokens.shape, bf16), in_specs...]
where the time goes in v4:
time: 70 us; the launch traced here: 69.9 us
  Pallas kernels  69.3 us (99%)
    pallas_call x1, Pallas kernels, feed_forward(): pl.pallas_call(kernel, out_shape=pltpu.VMEM(tokens.shape, bf16), in_specs...  69.3 us

profile of v4, /device:TPU:1, one launch (start us, length us, event | category | flops | bytes accessed | tf_op | source)
XLA Modules:
  0.0 69.9 jit_solution(3147792599499095756)
XLA Ops:
  0.0 69.3 %shard_map.73 = bf16[16,2048]{1,0:T(8,128)(2,1)S(1)} custom-call(bf16[16,2048]{1,0:T(8,128)(2,1)} %tokens.1, bf16[2048,896]{1,0:T(8,128)(2,1)} %gate_codes.1, f32[7,16]{1,0:T(8,128)} %bitcast.2, bf16[2048,896]{1,0:T(8,128)(2,1)} %up_codes.1, f32[7,16]{1,0:T(8,128)} %bitcast.3, bf16[896,2048]{1,0:T(8,128)(2,1)} %down_codes.1, f32[7,16]{1,0:T(8,128)} %down_scale.1), custom_call_target="tpu_custom_call" | custom-call | tf_op jit(solution)/shard_map/pallas_call | solution.py:320
  69.3 0.6 copy.9

commit v5 on v4

--- a/solution.py
+++ b/solution.py
@@ -54,7 +54,7 @@
 
     barrier = pltpu.get_barrier_semaphore()
     partners = [at_z(step) for step in (1, -1, 2, -2)]
-    partners += [side, twin, across, *pairs, *diagonals]
+    partners += [side, twin, across, *pairs]
     for partner in partners:
         pl.semaphore_signal(barrier, inc=1, device_id=partner, device_id_type=MESH)
     pl.semaphore_wait(barrier, len(partners))
@@ -161,6 +161,7 @@
     def scatter(unit):
         for stream in range(2):
             halves[unit, stream].wait_recv()
+        for stream in range(2):
             cut = both(stream)
             for index, (other_x, other_y, device) in enumerate(trio(unit, stream)):
                 send2[unit, index, :, cut] = partial(unit, stream, other_x, other_y).astype(

time: 70 us -> 68.8 us (0.983)
  Pallas kernels: 69.3 us -> 68 us
    pallas_call x1, Pallas kernels: 69.3 us -> 68 us  [feed_forward(): pl.pallas_call(kernel, out_shape=pltpu.VMEM(tokens.shape, bf16), in_specs...]
where the time goes in v5:
time: 68.8 us; the launch traced here: 68.7 us
  Pallas kernels  68 us (99%)
    pallas_call x1, Pallas kernels, feed_forward(): pl.pallas_call(kernel, out_shape=pltpu.VMEM(tokens.shape, bf16), in_specs...  68 us

profile of v5, /device:TPU:1, one launch (start us, length us, event | category | flops | bytes accessed | tf_op | source)
XLA Modules:
  0.0 68.7 jit_solution(2430199136894003722)
XLA Ops:
  0.0 68.0 %shard_map.73 = bf16[16,2048]{1,0:T(8,128)(2,1)S(1)} custom-call(bf16[16,2048]{1,0:T(8,128)(2,1)} %tokens.1, bf16[2048,896]{1,0:T(8,128)(2,1)} %gate_codes.1, f32[7,16]{1,0:T(8,128)} %bitcast.2, bf16[2048,896]{1,0:T(8,128)(2,1)} %up_codes.1, f32[7,16]{1,0:T(8,128)} %bitcast.3, bf16[896,2048]{1,0:T(8,128)(2,1)} %down_codes.1, f32[7,16]{1,0:T(8,128)} %down_scale.1), custom_call_target="tpu_custom_call" | custom-call | tf_op jit(solution)/shard_map/pallas_call | solution.py:321
  68.1 0.6 copy.9
